TPU v7x, 128 devices: a whole 4x4x4 slice. The times are simulated.
128 devices in a mesh: node: 16 (over z_hi, x, core), local: 8 (over z_lo, y).
Axes of the slice: x: 4, y: 4, z: 4 (z_hi: 2, z_lo: 2; z = z_hi * 2 + z_lo), core: 2. Of those that a mesh axis runs over, the one named last changes fastest.
Arguments:
- image_embed: float32 [40960, 1152], P(('node', 'local')), may hold values from -1 to 1
- text_embed: float32 [40960, 1152], P(('node', 'local')), may hold values from -1 to 1
- logit_scale: float32 [], replicated, may hold values from 8 to 16
- logit_bias: float32 [], replicated, may hold values from -7 to -4
Outputs:
- image_grad: float32 [40960, 1152], P(('node', 'local'))
- text_grad: float32 [40960, 1152], P(('node', 'local'))
All inputs are finite; a program needn't handle non-finite values.
Results may differ from a plain program's by a relative error of at most 0.0014.
Values may be sent and summed in bfloat16 or wider, within the bound.
A program may use at most 128 MiB of HBM per device.

v0:
```python
import jax
import jax.numpy as jnp
from jax import lax
from jax.sharding import PartitionSpec as P


def shifted(array, axis, by):
    devices = lax.axis_size(axis)
    return lax.ppermute(array, axis, [(i, (i + by) % devices) for i in range(devices)])


def coefficients(image_half, block, own_local, logit_scale, logit_bias):
    logits = (
        logit_scale
        * lax.dot_general(
            image_half, block, (((1,), (1,)), ((), ())), preferred_element_type=jnp.float32
        )
        + logit_bias
    )
    group = block.shape[0] // 2
    image_ids = group + own_local + lax.iota(jnp.int32, image_half.shape[0])
    text_ids = lax.iota(jnp.int32, block.shape[0])
    match = (image_ids[:, None] == text_ids[None, :]).astype(jnp.float32)
    return (logit_scale * (jax.nn.sigmoid(logits) - match)).astype(jnp.bfloat16)


def per_device(image_embed, text_embed, logit_scale, logit_bias):
    image_half = image_embed.astype(jnp.bfloat16)
    text_half = text_embed.astype(jnp.bfloat16)
    pair_rows = image_half.shape[0]
    own_local = lax.axis_index("local") * pair_rows
    group = lax.all_gather(text_half, "local", axis=0, tiled=True)
    before = shifted(group, "node", 1)
    block = jnp.concatenate([before, group], axis=0)
    coef = coefficients(image_half, block, own_local, logit_scale, logit_bias)
    image_grad = jnp.dot(coef, block, preferred_element_type=jnp.float32)
    text_part = lax.dot_general(
        coef, image_half, (((0,), (0,)), ((), ())), preferred_element_type=jnp.float32
    )
    span = group.shape[0]
    returned = shifted(text_part[:span], "node", -1)
    text_grad = lax.psum_scatter(
        text_part[span:] + returned, "local", scatter_dimension=0, tiled=True
    )
    return (image_grad, text_grad)


def solution(mesh):
    placed = (P(("node", "local"), None), P(("node", "local"), None), P(), P())
    return jax.shard_map(
        per_device,
        mesh=mesh,
        in_specs=placed,
        out_specs=(P(("node", "local"), None), P(("node", "local"), None)),
        check_vma=False,
    )
```

profile of v0, /device:TPU:0, one launch (start us, length us, event | category | flops | bytes accessed | tf_op | source)
XLA Modules:
  0.0 454.0 jit_solution(10889955967287799810)
XLA Ops:
  7.2 0.0 all-gather.2.cloned.1.call-start
  7.2 2.3 convert_element_type.12
  9.5 0.0 all-gather.2.cloned.1.call-update
  9.5 0.0 reduce-scatter.2.cloned.1.call-start
  9.6 71.8 %all-gather.2.cloned.1.call-done = bf16[2560,1152]{1,0:T(8,128)(2,1)} async-done(((bf16[320,1152]{1,0:T(8,128)(2,1)}), bf16[2560,1152]{1,0:T(8,128)(2,1)}) %all-gather.2.cloned.1.call-update) | async-done | bytes 5898256 | tf_op jit(solution)/shard_map/all_gather | solution.py:32
  81.4 0.0 slice-start
  81.4 0.0 collective-permute-start
  82.8 0.0 slice-start.1
  82.8 68.7 %collective-permute-done = bf16[2560,1152]{1,0:T(8,128)(2,1)} collective-permute-done((bf16[2560,1152]{1,0:T(8,128)(2,1)}, bf16[2560,1152]{1,0:T(8,128)(2,1)}, u32[]{:S(2)}, u32[]{:S(2)}) %collective-permute-start) | collective-permute-done | bytes 5898272 | tf_op jit(solution)/shard_map/ppermute | solution.py:9
  151.5 3.1 constant_dynamic-update-slice_fusion.1
  154.6 0.0 slice-done
  154.6 0.0 slice-done.1
  154.6 0.9 constant_dynamic-update-slice_fusion
  155.5 0.0 copy-start
  155.6 0.0 copy-start.1
  155.6 8.4 %fusion.1 = bf16[320,5120]{1,0:T(8,128)(2,1)S(1)} fusion(bf16[5120,1152]{1,0:T(8,128)(2,1)S(1)} %constant_dynamic-update-slice_fusion, s32[320]{0:T(512)S(1)} %iota_add_fusion, f32[]{:T(128)S(6)} %copy.8, f32[]{:T(128)S(6)} %copy.7, f32[320,1152]{1,0:T(8,128)} %param.4), kind=kOutput, calls=%fused_computation.4 | convolution fusion | flops 3791626240 | bytes 16549128 | tf_op jit(solution)/shard_map/dot_general | solution.py:15
  164.0 0.0 copy-done
  164.0 0.0 copy-done.1
  164.0 11.3 %fusion.2 = f32[5120,1152]{1,0:T(8,128)} fusion(bf16[320,5120]{1,0:T(8,128)(2,1)S(1)} %fusion.1, f32[320,1152]{1,0:T(8,128)S(1)} %copy-done.1), kind=kOutput, calls=%fused_computation.6 | convolution fusion | flops 3775242240 | bytes 28344320 | tf_op jit(solution)/shard_map/dot_general | solution.py:37
  175.3 9.4 %slice.9 = f32[2560,1152]{1,0:T(8,128)} slice(f32[5120,1152]{1,0:T(8,128)} %fusion.2), slice={[0:2560], [0:1152]} | slice | bytes 23592960 | tf_op jit(solution)/shard_map/slice | solution.py:41
  184.7 0.0 collective-permute-start.1
  184.8 127.8 %collective-permute-done.1 = f32[2560,1152]{1,0:T(8,128)S(1)} collective-permute-done((f32[2560,1152]{1,0:T(8,128)}, f32[2560,1152]{1,0:T(8,128)S(1)}, u32[]{:S(2)}, u32[]{:S(2)}) %collective-permute-start.1) | collective-permute-done | bytes 11796512 | tf_op jit(solution)/shard_map/ppermute | solution.py:9
  312.5 10.3 %slice_add_fusion = f32[2560,1152]{1,0:T(8,128)} fusion(f32[2560,1152]{1,0:T(8,128)S(1)} %collective-permute-done.1, f32[5120,1152]{1,0:T(8,128)} %fusion.2), kind=kLoop, calls=%fused_computation | loop fusion | flops 2949120 | bytes 35389440 | tf_op jit(solution)/shard_map/add | solution.py:43
  322.8 0.0 reduce-scatter.2.cloned.1.call-update
  322.8 8.4 %fusion.5 = f32[320,1152]{1,0:T(8,128)} fusion(bf16[320,5120]{1,0:T(8,128)(2,1)S(1)} %fusion.1, bf16[5120,1152]{1,0:T(8,128)(2,1)} %copy-done), kind=kOutput, calls=%fused_computation.12 | convolution fusion | flops 3774873600 | bytes 16547840 | tf_op jit(solution)/shard_map/dot_general | solution.py:36
  331.2 116.0 %reduce-scatter.2.cloned.1.call-done = f32[320,1152]{1,0:T(8,128)} async-done(((f32[2560,1152]{1,0:T(8,128)}), f32[320,1152]{1,0:T(8,128)}) %reduce-scatter.2.cloned.1.call-update) | async-done | bytes 1474576 | tf_op jit(solution)/shard_map/reduce_scatter | solution.py:42
  (2 shorter events, 0.0 us)
Async XLA Ops:
  7.2 74.2 %all-gather.2.cloned.1.call-start = ((), (), s32[]{:S(2)}) async-start(), calls=%async_computation.1 | async-start | bytes 6635520 | tf_op jit(solution)/shard_map/all_gather | solution.py:32
  9.5 437.7 %reduce-scatter.2.cloned.1.call-start = ((), (), s32[]{:S(2)}) async-start(), calls=%async_computation.2 | async-start | bytes 13271040 | tf_op jit(solution)/shard_map/reduce_scatter | solution.py:42
  81.4 73.2 %slice-start = ((s8[5898240]{0:T(1024)(128)(4,1)}), s8[1703936]{0:T(1024)(128)(4,1)S(1)}, s32[]{:S(2)}) async-start(s8[5898240]{0:T(1024)(128)(4,1)} %bitcast.10), calls=%async_computation.3 | async-start | bytes 3407872
  81.4 70.1 %collective-permute-start = (bf16[2560,1152]{1,0:T(8,128)(2,1)}, bf16[2560,1152]{1,0:T(8,128)(2,1)}, u32[]{:S(2)}, u32[]{:S(2)}) collective-permute-start(bf16[2560,1152]{1,0:T(8,128)(2,1)} %all-gather.2.cloned.1.call-done), channel_id=1, source_target_pairs={{0,8},{8,16},{16,24},{24,32},{32,40},{40,48},{48,56},{56,64},{64,7... | collective-permute-start | bytes 17694728 | tf_op jit(solution)/shard_map/ppermute | solution.py:9
  82.8 71.8 %slice-start.1 = ((s8[5898240]{0:T(1024)(128)(4,1)}), s8[4194304]{0:T(1024)(128)(4,1)S(1)}, s32[]{:S(2)}) async-start(s8[5898240]{0:T(1024)(128)(4,1)} %bitcast.10), calls=%async_computation.4 | async-start | bytes 8388608
  155.5 8.4 %copy-start = (bf16[5120,1152]{1,0:T(8,128)(2,1)}, bf16[5120,1152]{1,0:T(8,128)(2,1)S(1)}, u32[]{:S(2)}) copy-start(bf16[5120,1152]{1,0:T(8,128)(2,1)S(1)} %constant_dynamic-update-slice_fusion) | copy-start | bytes 35389444
  155.6 8.4 %copy-start.1 = (f32[320,1152]{1,0:T(8,128)S(1)}, f32[320,1152]{1,0:T(8,128)}, u32[]{:S(2)}) copy-start(f32[320,1152]{1,0:T(8,128)} %param.4) | copy-start | bytes 4423684
  184.7 127.8 %collective-permute-start.1 = (f32[2560,1152]{1,0:T(8,128)}, f32[2560,1152]{1,0:T(8,128)S(1)}, u32[]{:S(2)}, u32[]{:S(2)}) collective-permute-start(f32[2560,1152]{1,0:T(8,128)} %slice.9), channel_id=1, source_target_pairs={{0,120},{8,0},{16,8},{24,16},{32,24},{40,32},{48,40},{56,48},{64,5... | collective-permute-start | bytes 35389448 | tf_op jit(solution)/shard_map/ppermute | solution.py:9
Sparse Core Ops, SparseCore 0:
  10.2 71.1 all-gather.1
  322.9 124.2 reduce-scatter.1
where the time goes:
time: 455 us; the launch traced here: 454 us
  waiting for transfers between devices  384 us (84%)
  matrix products  28.1 us (6%)
  between operations  15.6 us (3%)
  local copies, waits for them, and re-layouts  13.5 us (3%)
  other arithmetic  12.6 us (3%)
    ppermute x2, waiting for transfers between devices, shifted(): lax.ppermute(array, axis, [(i, (i + by) % devices) for i in range(devices)])  196 us
    reduce_scatter x1, waiting for transfers between devices, per_device(): lax.psum_scatter(text_part[span:] + returned, 'local', scatter_dimension=...  116 us
    all_gather x1, waiting for transfers between devices, per_device(): group = lax.all_gather(text_half, 'local', axis=0, tiled=True)  71.8 us
    dot_general x1, matrix products, per_device(): lax.dot_general(coef, image_half, (((0,), (0,)), ((), ())), preferred_ele...  11.3 us
    add x1, other arithmetic, per_device(): text_part[span:] + returned  10.3 us
    slice x1, local copies, waits for them, and re-layouts, per_device(): returned = shifted(text_part[:span], 'node', -1)  9.43 us
  transfers between devices with their start and end apart: 4, of which 4 were waited for; matrix products, arithmetic and copies ran while one was open for 2% of the time, Pallas kernels for 0%

commit v1 on v0

v1 whole, which is shorter than its diff:
```python
import jax
import jax.numpy as jnp
from jax import lax
from jax.experimental import pallas as pl
from jax.experimental.pallas import tpu as pltpu
from jax.sharding import PartitionSpec as P

MESH = pl.DeviceIdType.MESH
ROWS, WIDTH = 320, 1152
HALF, PIECE = ROWS // 2, ROWS // 4
BLOCK = 4 * ROWS
NT = (((1,), (1,)), ((), ()))
TN = (((0,), (0,)), ((), ()))


def neighbours():
    node, local = lax.axis_index("node"), lax.axis_index("local")
    z_hi, x, core = node // 8, (node // 2) % 4, node % 2
    z_lo, y = local // 4, local % 4
    right = (node, z_lo * 4 + (y + 1) % 4)
    left = (node, z_lo * 4 + (y + 3) % 4)
    partner = (node, (1 - z_lo) * 4 + y)
    first = jnp.logical_and(core == 0, x == 0)
    last = jnp.logical_and(core == 1, x == 3)
    flipped = (1 - z_lo) * 4 + y
    before = ((node + 15) % 16, jnp.where(first, flipped, local))
    after = ((node + 1) % 16, jnp.where(last, flipped, local))
    return right, left, partner, before, after


def packed(value):
    square = value * value
    return (square * (value * jnp.abs(value))).astype(jnp.bfloat16)


def unpacked(power):
    power = power.astype(jnp.float32)
    root = lax.rsqrt(jnp.maximum(jnp.abs(power), 1e-37))
    return (power * root) * (root * lax.rsqrt(root))


def kernel(
    scale_ref, bias_ref, image_hbm, text_hbm, image_out, text_out,
    image_in, text_in, texts, images, coef, text_part, image_part,
    text_send, image_send, mid_recv, right_recv, left_recv, zn_recv, dn_recv, z_recv,
    image_sum, text_sum, load_sem, store_sem, send_sem, recv_sem,
):
    right, left, partner, before, after = neighbours()
    scale, bias = scale_ref[0], bias_ref[0]
    load_text = pltpu.make_async_copy(text_hbm, text_in, load_sem.at[0])
    load_image = pltpu.make_async_copy(image_hbm, image_in, load_sem.at[1])
    load_text.start()
    load_image.start()
    barrier = pltpu.get_barrier_semaphore()
    for device in (right, left, partner, before, after):
        pl.semaphore_signal(barrier, 1, device_id=device, device_id_type=MESH)

    copies = []

    def send(device, source, source_row, target, target_row, rows):
        k = len(copies)
        copy = pltpu.make_async_remote_copy(
            src_ref=source.at[pl.ds(source_row, rows)],
            dst_ref=target.at[pl.ds(target_row, rows)],
            send_sem=send_sem.at[k],
            recv_sem=recv_sem.at[k],
            device_id=device,
            device_id_type=MESH,
        )
        copy.start()
        copies.append(copy)
        return copy

    def coefficients(group, pair):
        block = texts[pl.ds(group * ROWS, ROWS), :]
        logits = scale * lax.dot_general(
            block, images[pl.ds(pair * 2 * ROWS, 2 * ROWS), :], NT, preferred_element_type=jnp.float32
        ) + bias
        value = 1.0 / (1.0 + jnp.exp(-logits))
        if group == 0 and pair == 0:
            shape = (ROWS, 2 * ROWS)
            match = lax.broadcasted_iota(jnp.int32, shape, 0) == lax.broadcasted_iota(jnp.int32, shape, 1)
            value = value - match.astype(jnp.float32)
        coef[pl.ds(group * ROWS, ROWS), pl.ds(pair * 2 * ROWS, 2 * ROWS)] = (scale * value).astype(jnp.bfloat16)

    def text_rows(group):
        rows = pl.ds(group * ROWS, ROWS)
        text_part[rows, :] = jnp.dot(coef[rows, :], images[...], preferred_element_type=jnp.float32)

    def image_rows(pair):
        lanes = pl.ds(pair * 2 * ROWS, 2 * ROWS)
        image_part[lanes, :] = lax.dot_general(coef[:, lanes], texts[...], TN, preferred_element_type=jnp.float32)

    def pack_text(row, rows):
        text_send[pl.ds(row - ROWS, rows), :] = packed(text_part[pl.ds(row, rows), :])

    load_text.wait()
    texts[pl.ds(0, ROWS), :] = text_in[...].astype(jnp.bfloat16)
    pl.semaphore_wait(barrier, 5)
    y_near = []
    for i in range(2):
        y_near.append((
            send(right, texts, PIECE * i, texts, 320 + PIECE * i, PIECE),
            send(left, texts, HALF + PIECE * i, texts, 480 + PIECE * i, PIECE),
        ))
    load_image.wait()
    images[pl.ds(0, ROWS), :] = image_in[...].astype(jnp.bfloat16)
    z_image = [send(partner, images, PIECE * i, images, 640 + PIECE * i, PIECE) for i in range(4)]
    n_image = send(before, images, 0, images, 320, ROWS)

    y_far, nz_image = [], []

    def forward_y(i):
        y_near[i][0].wait_recv()
        a = send(right, texts, 320 + PIECE * i, texts, 640 + PIECE * i, PIECE)
        y_near[i][1].wait_recv()
        b = send(left, texts, 480 + PIECE * i, texts, 800 + PIECE * i, PIECE)
        y_far.append((a, b))

    def forward_z(i):
        z_image[i].wait_recv()
        nz_image.append(send(before, images, 640 + PIECE * i, images, 960 + PIECE * i, PIECE))

    forward_y(0)
    forward_z(0)
    forward_y(1)
    y_last = (send(right, texts, HALF, texts, 960, HALF), send(left, texts, 0, texts, 1120, HALF))
    forward_z(1)
    n_image.wait_recv()
    coefficients(0, 0)
    coefficients(1, 0)
    forward_z(2)
    for i in range(2):
        for copy in y_far[i]:
            copy.wait_recv()
    forward_z(3)
    coefficients(2, 0)
    for copy in nz_image:
        copy.wait_recv()

    coefficients(1, 1)
    text_rows(1)
    pack_text(320, ROWS)
    near = [(send(left, text_send, 0, right_recv, 0, PIECE), send(right, text_send, 160, left_recv, 160, PIECE))]
    coefficients(2, 1)
    text_rows(2)
    pack_text(640, ROWS)
    mid = []
    for i in range(2):
        mid.append((
            send(left, text_send, 480 + PIECE * i, mid_recv, PIECE * i, PIECE),
            send(right, text_send, 320 + PIECE * i, mid_recv, HALF + PIECE * i, PIECE),
        ))
    near.append((send(left, text_send, PIECE, right_recv, PIECE, PIECE), send(right, text_send, 240, left_recv, 240, PIECE)))
    coefficients(0, 1)
    for copy in y_last:
        copy.wait_recv()
    coefficients(3, 1)
    coefficients(3, 0)
    image_rows(1)
    image_send[pl.ds(640, ROWS), :] = packed(image_part[pl.ds(960, ROWS), :])
    nz_part = [send(after, image_send, 640 + PIECE * i, zn_recv, PIECE * i, PIECE) for i in range(4)]
    image_rows(0)
    image_send[pl.ds(0, ROWS), :] = packed(image_part[pl.ds(320, ROWS), :])
    n_part = send(after, image_send, 0, dn_recv, 0, ROWS)
    text_rows(3)
    text_rows(0)

    z_part, last = [], []

    def reduce_z(i):
        nz_part[i].wait_recv()
        rows = pl.ds(PIECE * i, PIECE)
        image_send[pl.ds(320 + PIECE * i, PIECE), :] = packed(
            image_part[pl.ds(640 + PIECE * i, PIECE), :] + unpacked(zn_recv[rows, :])
        )
        z_part.append(send(partner, image_send, 320 + PIECE * i, z_recv, PIECE * i, PIECE))

    def reduce_y(i):
        pair = []
        for k, device, target, target_row in ((0, left, right_recv, HALF), (1, right, left_recv, 0)):
            mid[i][k].wait_recv()
            row = HALF * k + PIECE * i
            text_send[pl.ds(640 + row, PIECE), :] = packed(
                text_part[pl.ds(960 + row, PIECE), :] + unpacked(mid_recv[pl.ds(row, PIECE), :])
            )
            pair.append(send(device, text_send, 640 + row, target, target_row + PIECE * i, PIECE))
        last.append(pair)

    reduce_z(0)
    reduce_z(1)
    reduce_y(0)
    reduce_z(2)
    reduce_z(3)
    reduce_y(1)

    n_part.wait_recv()
    image_sum[...] = image_part[pl.ds(0, ROWS), :] + unpacked(dn_recv[...])
    stores = []

    def store(source, target, row, rows):
        copy = pltpu.make_async_copy(
            source.at[pl.ds(row, rows)], target.at[pl.ds(row, rows)], store_sem.at[len(stores)]
        )
        copy.start()
        stores.append(copy)

    for i in range(2):
        for j in (2 * i, 2 * i + 1):
            z_part[j].wait_recv()
        rows = pl.ds(HALF * i, HALF)
        image_sum[rows, :] += unpacked(z_recv[rows, :])
        store(image_sum, image_out, HALF * i, HALF)
    for pair in near:
        for copy in pair:
            copy.wait_recv()
    text_sum[pl.ds(0, HALF), :] = text_part[pl.ds(0, HALF), :] + unpacked(right_recv[pl.ds(0, HALF), :])
    text_sum[pl.ds(HALF, HALF), :] = text_part[pl.ds(HALF, HALF), :] + unpacked(left_recv[pl.ds(HALF, HALF), :])
    for i in range(2):
        for k, source, row in ((0, right_recv, HALF), (1, left_recv, 0)):
            last[i][k].wait_recv()
            rows = pl.ds(row + PIECE * i, PIECE)
            text_sum[rows, :] += unpacked(source[rows, :])
            store(text_sum, text_out, row + PIECE * i, PIECE)
    for copy in copies:
        copy.wait_send()
    for copy in stores:
        copy.wait()


def per_device(image_embed, text_embed, logit_scale, logit_bias):
    half = lambda rows: pltpu.VMEM((rows, WIDTH), jnp.bfloat16)
    full = lambda rows: pltpu.VMEM((rows, WIDTH), jnp.float32)
    n_copies = 48
    out = jax.ShapeDtypeStruct((ROWS, WIDTH), jnp.float32)
    return pl.pallas_call(
        kernel,
        out_shape=(out, out),
        in_specs=[pl.BlockSpec(memory_space=pltpu.SMEM)] * 2 + [pl.BlockSpec(memory_space=pl.ANY)] * 2,
        out_specs=(pl.BlockSpec(memory_space=pl.ANY),) * 2,
        scratch_shapes=[
            full(ROWS), full(ROWS), half(BLOCK), half(BLOCK), pltpu.VMEM((BLOCK, BLOCK), jnp.bfloat16),
            full(BLOCK), full(BLOCK),
            half(3 * ROWS), half(3 * ROWS), half(ROWS), half(ROWS), half(ROWS), half(ROWS), half(ROWS), half(ROWS),
            full(ROWS), full(ROWS),
            pltpu.SemaphoreType.DMA((2,)), pltpu.SemaphoreType.DMA((6,)),
            pltpu.SemaphoreType.DMA((n_copies,)), pltpu.SemaphoreType.DMA((n_copies,)),
        ],
        compiler_params=pltpu.CompilerParams(
            collective_id=0, has_side_effects=True, vmem_limit_bytes=60 * 2**20
        ),
        cost_estimate=pl.CostEstimate(
            flops=6 * BLOCK * BLOCK * WIDTH, bytes_accessed=16 * ROWS * WIDTH, transcendentals=BLOCK * BLOCK
        ),
    )(logit_scale.reshape(1), logit_bias.reshape(1), image_embed, text_embed)


def solution(mesh):
    placed = (P(("node", "local"), None), P(("node", "local"), None), P(), P())
    return jax.shard_map(
        per_device,
        mesh=mesh,
        in_specs=placed,
        out_specs=(P(("node", "local"), None), P(("node", "local"), None)),
        check_vma=False,
    )
```

time: 455 us -> 69.6 us (0.15)
  waiting for transfers between devices: 384 us -> 0 us
  Pallas kernels: 0 us -> 63.7 us
  matrix products: 28.1 us -> 0 us
  between operations: 15.6 us -> 1.94 us
  other arithmetic: 12.6 us -> 0 us
  local copies, waits for them, and re-layouts: 13.5 us -> 3.8 us
    ppermute x2 -> x0, waiting for transfers between devices: 196 us -> none  [shifted(): lax.ppermute(array, axis, [(i, (i + by) % devices) for i in range(devices)])]
    reduce_scatter x1 -> x0, waiting for transfers between devices: 116 us -> none  [per_device(): lax.psum_scatter(text_part[span:] + returned, 'local', scatter_dimension=...]
    all_gather x1 -> x0, waiting for transfers between devices: 71.8 us -> none  [per_device(): group = lax.all_gather(text_half, 'local', axis=0, tiled=True)]
    pallas_call x0 -> x1, Pallas kernels: none -> 63.7 us  [per_device(): pl.pallas_call(kernel, out_shape=(out, out), in_specs=[pl.BlockSpec(memor...]
    dot_general x3 -> x0, matrix products: 28.1 us -> none  [the longest x1 11.3 us: per_device(): lax.dot_general(coef, image_half, (((0,), (0,)), ((), ())), preferred_ele...]
    add x2 -> x0, other arithmetic: 10.3 us -> none  [the longest x1 10.3 us: per_device(): text_part[span:] + returned]
    slice x1 -> x0, local copies, waits for them, and re-layouts: 9.43 us -> none  [per_device(): returned = shifted(text_part[:span], 'node', -1)]
  transfers between devices with their start and end apart: 4 -> 0, of which waited for: 4 -> 0; matrix products, arithmetic and copies ran while one was open for 2% -> 0% of each run, Pallas kernels for 0% -> 0%
where the time goes in v1:
time: 69.6 us; the launch traced here: 69.4 us
  Pallas kernels  63.7 us (92%)
  local copies, waits for them, and re-layouts  3.8 us (5%)
  between operations  1.94 us (3%)
    pallas_call x1, Pallas kernels, per_device(): pl.pallas_call(kernel, out_shape=(out, out), in_specs=[pl.BlockSpec(memor...  63.7 us
    unnamed x4, local copies, waits for them, and re-layouts  3.8 us

profile of v1, /device:TPU:0, one launch (start us, length us, event | category | flops | bytes accessed | tf_op | source)
XLA Modules:
  0.0 69.4 jit_solution(18220667835366882149)
XLA Ops:
  1.9 63.7 %shard_map.59 = (f32[320,1152]{1,0:T(8,128)}, f32[320,1152]{1,0:T(8,128)}) custom-call(f32[1]{0:T(128)} %bitcast.2.scale_ref, f32[1]{0:T(128)} %bitcast.3.bias_ref, f32[320,1152]{1,0:T(8,128)} %image_hbm.1, f32[320,1152]{1,0:T(8,128)} %text_hbm.1), custom_call_target="tpu_custom_call" | custom-call | flops 11324620800 | bytes 5898240 | tf_op jit(solution)/shard_map/pallas_call | solution.py:236
  65.6 0.0 copy-start
  65.6 2.7 %copy.10 = f32[320,1152]{1,0:T(8,128)} copy(f32[320,1152]{1,0:T(8,128)} %get-tuple-element.4) | data formatting | bytes 2949120
  68.3 0.0 copy-done
  68.3 1.1 %copy.11 = f32[320,1152]{1,0:T(8,128)} copy(f32[320,1152]{1,0:T(8,128)S(1)} %copy-done) | data formatting | bytes 2949120
Async XLA Ops:
  65.6 2.7 %copy-start = (f32[320,1152]{1,0:T(8,128)S(1)}, f32[320,1152]{1,0:T(8,128)}, u32[]{:S(2)}) copy-start(f32[320,1152]{1,0:T(8,128)} %get-tuple-element.5) | copy-start | bytes 4423684

commit v2 on v1

--- a/solution.py
+++ b/solution.py
@@ -43,9 +43,10 @@
     scale_ref, bias_ref, image_hbm, text_hbm, image_out, text_out,
     image_in, text_in, texts, images, coef, text_part, image_part,
     text_send, image_send, mid_recv, right_recv, left_recv, zn_recv, dn_recv, z_recv,
-    image_sum, text_sum, load_sem, store_sem, send_sem, recv_sem,
+    load_sem, send_sem, recv_sem,
 ):
     right, left, partner, before, after = neighbours()
+    core = lax.axis_index("node") % 2
     scale, bias = scale_ref[0], bias_ref[0]
     load_text = pltpu.make_async_copy(text_hbm, text_in, load_sem.at[0])
     load_image = pltpu.make_async_copy(image_hbm, image_in, load_sem.at[1])
@@ -57,7 +58,7 @@
 
     copies = []
 
-    def send(device, source, source_row, target, target_row, rows):
+    def send(device, source, source_row, target, target_row, rows, start=True):
         k = len(copies)
         copy = pltpu.make_async_remote_copy(
             src_ref=source.at[pl.ds(source_row, rows)],
@@ -67,8 +68,9 @@
             device_id=device,
             device_id_type=MESH,
         )
-        copy.start()
         copies.append(copy)
+        if start:
+            copy.start()
         return copy
 
     def coefficients(group, pair):
@@ -87,15 +89,23 @@
         rows = pl.ds(group * ROWS, ROWS)
         text_part[rows, :] = jnp.dot(coef[rows, :], images[...], preferred_element_type=jnp.float32)
 
-    def image_rows(pair):
+    def image_rows(pair, first, rows):
         lanes = pl.ds(pair * 2 * ROWS, 2 * ROWS)
-        image_part[lanes, :] = lax.dot_general(coef[:, lanes], texts[...], TN, preferred_element_type=jnp.float32)
+        part = lax.dot_general(
+            coef[pl.ds(first, rows), lanes], texts[pl.ds(first, rows), :], TN, preferred_element_type=jnp.float32
+        )
+        if first:
+            image_part[lanes, :] += part
+        else:
+            image_part[lanes, :] = part
 
     def pack_text(row, rows):
         text_send[pl.ds(row - ROWS, rows), :] = packed(text_part[pl.ds(row, rows), :])
 
     load_text.wait()
     texts[pl.ds(0, ROWS), :] = text_in[...].astype(jnp.bfloat16)
+    load_image.wait()
+    images[pl.ds(0, ROWS), :] = image_in[...].astype(jnp.bfloat16)
     pl.semaphore_wait(barrier, 5)
     y_near = []
     for i in range(2):
@@ -103,12 +113,25 @@
             send(right, texts, PIECE * i, texts, 320 + PIECE * i, PIECE),
             send(left, texts, HALF + PIECE * i, texts, 480 + PIECE * i, PIECE),
         ))
-    load_image.wait()
-    images[pl.ds(0, ROWS), :] = image_in[...].astype(jnp.bfloat16)
-    z_image = [send(partner, images, PIECE * i, images, 640 + PIECE * i, PIECE) for i in range(4)]
+    z_image = [send(partner, images, PIECE * i, images, 640 + PIECE * i, PIECE, False) for i in range(4)]
+    nz_image = [send(before, images, 640 + PIECE * i, images, 960 + PIECE * i, PIECE, False) for i in range(4)]
+
+    def start_z(which):
+        @pl.when(core == which)
+        def _():
+            for copy in z_image:
+                copy.start()
+
+    def forward_z(which, pieces):
+        @pl.when(core == which)
+        def _():
+            for i in pieces:
+                z_image[i].wait_recv()
+                nz_image[i].start()
+
+    start_z(0)
     n_image = send(before, images, 0, images, 320, ROWS)
-
-    y_far, nz_image = [], []
+    y_far = []
 
     def forward_y(i):
         y_near[i][0].wait_recv()
@@ -117,23 +140,22 @@
         b = send(left, texts, 480 + PIECE * i, texts, 800 + PIECE * i, PIECE)
         y_far.append((a, b))
 
-    def forward_z(i):
-        z_image[i].wait_recv()
-        nz_image.append(send(before, images, 640 + PIECE * i, images, 960 + PIECE * i, PIECE))
-
     forward_y(0)
-    forward_z(0)
+    start_z(1)
+    forward_z(0, (0, 1))
     forward_y(1)
     y_last = (send(right, texts, HALF, texts, 960, HALF), send(left, texts, 0, texts, 1120, HALF))
-    forward_z(1)
+    forward_z(0, (2, 3))
     n_image.wait_recv()
     coefficients(0, 0)
+    forward_z(1, (0,))
     coefficients(1, 0)
-    forward_z(2)
-    for i in range(2):
-        for copy in y_far[i]:
-            copy.wait_recv()
-    forward_z(3)
+    forward_z(1, (1, 2))
+    for copy in y_far[0]:
+        copy.wait_recv()
+    forward_z(1, (3,))
+    for copy in y_far[1]:
+        copy.wait_recv()
     coefficients(2, 0)
     for copy in nz_image:
         copy.wait_recv()
@@ -153,14 +175,15 @@
         ))
     near.append((send(left, text_send, PIECE, right_recv, PIECE, PIECE), send(right, text_send, 240, left_recv, 240, PIECE)))
     coefficients(0, 1)
+    image_rows(1, 0, 3 * ROWS)
     for copy in y_last:
         copy.wait_recv()
     coefficients(3, 1)
-    coefficients(3, 0)
-    image_rows(1)
+    image_rows(1, 3 * ROWS, ROWS)
     image_send[pl.ds(640, ROWS), :] = packed(image_part[pl.ds(960, ROWS), :])
     nz_part = [send(after, image_send, 640 + PIECE * i, zn_recv, PIECE * i, PIECE) for i in range(4)]
-    image_rows(0)
+    coefficients(3, 0)
+    image_rows(0, 0, BLOCK)
     image_send[pl.ds(0, ROWS), :] = packed(image_part[pl.ds(320, ROWS), :])
     n_part = send(after, image_send, 0, dn_recv, 0, ROWS)
     text_rows(3)
@@ -195,55 +218,41 @@
     reduce_y(1)
 
     n_part.wait_recv()
-    image_sum[...] = image_part[pl.ds(0, ROWS), :] + unpacked(dn_recv[...])
-    stores = []
-
-    def store(source, target, row, rows):
-        copy = pltpu.make_async_copy(
-            source.at[pl.ds(row, rows)], target.at[pl.ds(row, rows)], store_sem.at[len(stores)]
-        )
-        copy.start()
-        stores.append(copy)
-
+    image_out[...] = image_part[pl.ds(0, ROWS), :] + unpacked(dn_recv[...])
     for i in range(2):
         for j in (2 * i, 2 * i + 1):
             z_part[j].wait_recv()
         rows = pl.ds(HALF * i, HALF)
-        image_sum[rows, :] += unpacked(z_recv[rows, :])
-        store(image_sum, image_out, HALF * i, HALF)
+        image_out[rows, :] += unpacked(z_recv[rows, :])
     for pair in near:
         for copy in pair:
             copy.wait_recv()
-    text_sum[pl.ds(0, HALF), :] = text_part[pl.ds(0, HALF), :] + unpacked(right_recv[pl.ds(0, HALF), :])
-    text_sum[pl.ds(HALF, HALF), :] = text_part[pl.ds(HALF, HALF), :] + unpacked(left_recv[pl.ds(HALF, HALF), :])
+    text_out[pl.ds(0, HALF), :] = text_part[pl.ds(0, HALF), :] + unpacked(right_recv[pl.ds(0, HALF), :])
+    text_out[pl.ds(HALF, HALF), :] = text_part[pl.ds(HALF, HALF), :] + unpacked(left_recv[pl.ds(HALF, HALF), :])
     for i in range(2):
         for k, source, row in ((0, right_recv, HALF), (1, left_recv, 0)):
             last[i][k].wait_recv()
             rows = pl.ds(row + PIECE * i, PIECE)
-            text_sum[rows, :] += unpacked(source[rows, :])
-            store(text_sum, text_out, row + PIECE * i, PIECE)
+            text_out[rows, :] += unpacked(source[rows, :])
     for copy in copies:
         copy.wait_send()
-    for copy in stores:
-        copy.wait()
 
 
 def per_device(image_embed, text_embed, logit_scale, logit_bias):
     half = lambda rows: pltpu.VMEM((rows, WIDTH), jnp.bfloat16)
     full = lambda rows: pltpu.VMEM((rows, WIDTH), jnp.float32)
     n_copies = 48
-    out = jax.ShapeDtypeStruct((ROWS, WIDTH), jnp.float32)
+    out = pltpu.VMEM((ROWS, WIDTH), jnp.float32)
     return pl.pallas_call(
         kernel,
         out_shape=(out, out),
-        in_specs=[pl.BlockSpec(memory_space=pltpu.SMEM)] * 2 + [pl.BlockSpec(memory_space=pl.ANY)] * 2,
-        out_specs=(pl.BlockSpec(memory_space=pl.ANY),) * 2,
+        in_specs=[pl.BlockSpec(memory_space=pltpu.SMEM)] * 2 + [pl.BlockSpec(memory_space=pltpu.HBM)] * 2,
+        out_specs=(pl.BlockSpec(memory_space=pltpu.VMEM),) * 2,
         scratch_shapes=[
             full(ROWS), full(ROWS), half(BLOCK), half(BLOCK), pltpu.VMEM((BLOCK, BLOCK), jnp.bfloat16),
             full(BLOCK), full(BLOCK),
             half(3 * ROWS), half(3 * ROWS), half(ROWS), half(ROWS), half(ROWS), half(ROWS), half(ROWS), half(ROWS),
-            full(ROWS), full(ROWS),
-            pltpu.SemaphoreType.DMA((2,)), pltpu.SemaphoreType.DMA((6,)),
+            pltpu.SemaphoreType.DMA((2,)),
             pltpu.SemaphoreType.DMA((n_copies,)), pltpu.SemaphoreType.DMA((n_copies,)),
         ],
         compiler_params=pltpu.CompilerParams(

time: 69.6 us -> 65.1 us (0.935)
  Pallas kernels: 63.7 us -> 60.8 us
  local copies, waits for them, and re-layouts: 3.8 us -> 2.22 us
    pallas_call x1, Pallas kernels: 63.7 us -> 60.8 us  [per_device(): pl.pallas_call(kernel, out_shape=(out, out), in_specs=[pl.BlockSpec(memor...]
    unnamed x4 -> x2, local copies, waits for them, and re-layouts: 3.8 us -> 2.22 us
where the time goes in v2:
time: 65.1 us; the launch traced here: 65 us
  Pallas kernels  60.8 us (93%)
  local copies, waits for them, and re-layouts  2.22 us (3%)
  between operations  1.93 us (3%)
    pallas_call x1, Pallas kernels, per_device(): pl.pallas_call(kernel, out_shape=(out, out), in_specs=[pl.BlockSpec(memor...  60.8 us
    unnamed x2, local copies, waits for them, and re-layouts  2.22 us

profile of v2, /device:TPU:0, one launch (start us, length us, event | category | flops | bytes accessed | tf_op | source)
XLA Modules:
  0.0 65.0 jit_solution(16109018540931554934)
XLA Ops:
  1.9 60.8 %shard_map.59 = (f32[320,1152]{1,0:T(8,128)S(1)}, f32[320,1152]{1,0:T(8,128)S(1)}) custom-call(f32[1]{0:T(128)} %bitcast.2.scale_ref, f32[1]{0:T(128)} %bitcast.3.bias_ref, f32[320,1152]{1,0:T(8,128)} %image_hbm.1, f32[320,1152]{1,0:T(8,128)} %text_hbm.1), custom_call_target="tpu_custom_call" | custom-call | flops 11324620800 | bytes 5898240 | tf_op jit(solution)/shard_map/pallas_call | solution.py:246
  62.7 1.1 %copy.8 = f32[320,1152]{1,0:T(8,128)} copy(f32[320,1152]{1,0:T(8,128)S(1)} %get-tuple-element.2) | data formatting | bytes 2949120
  63.9 1.1 %copy.9 = f32[320,1152]{1,0:T(8,128)} copy(f32[320,1152]{1,0:T(8,128)S(1)} %get-tuple-element.3) | data formatting | bytes 2949120

commit v3 on v2

--- a/solution.py
+++ b/solution.py
@@ -73,31 +73,33 @@
             copy.start()
         return copy
 
-    def coefficients(group, pair):
-        block = texts[pl.ds(group * ROWS, ROWS), :]
+    def coefficients(group, lane, lanes):
+        rows, place = pl.ds(group * ROWS, ROWS), pl.ds(lane, lanes)
         logits = scale * lax.dot_general(
-            block, images[pl.ds(pair * 2 * ROWS, 2 * ROWS), :], NT, preferred_element_type=jnp.float32
+            texts[rows, :], images[place, :], NT, preferred_element_type=jnp.float32
         ) + bias
         value = 1.0 / (1.0 + jnp.exp(-logits))
-        if group == 0 and pair == 0:
-            shape = (ROWS, 2 * ROWS)
+        if group == 0 and lane == 0:
+            shape = (ROWS, lanes)
             match = lax.broadcasted_iota(jnp.int32, shape, 0) == lax.broadcasted_iota(jnp.int32, shape, 1)
             value = value - match.astype(jnp.float32)
-        coef[pl.ds(group * ROWS, ROWS), pl.ds(pair * 2 * ROWS, 2 * ROWS)] = (scale * value).astype(jnp.bfloat16)
-
-    def text_rows(group):
-        rows = pl.ds(group * ROWS, ROWS)
-        text_part[rows, :] = jnp.dot(coef[rows, :], images[...], preferred_element_type=jnp.float32)
-
-    def image_rows(pair, first, rows):
-        lanes = pl.ds(pair * 2 * ROWS, 2 * ROWS)
+        coef[rows, place] = (scale * value).astype(jnp.bfloat16)
+
+    def text_rows(group, pair):
+        rows, lanes = pl.ds(group * ROWS, ROWS), pl.ds(pair * 2 * ROWS, 2 * ROWS)
+        part = jnp.dot(coef[rows, lanes], images[lanes, :], preferred_element_type=jnp.float32)
+        if pair:
+            part = text_part[rows, :] + part
+        text_part[rows, :] = part
+
+    def image_rows(lane, lanes, first, rows):
+        place = pl.ds(lane, lanes)
         part = lax.dot_general(
-            coef[pl.ds(first, rows), lanes], texts[pl.ds(first, rows), :], TN, preferred_element_type=jnp.float32
+            coef[pl.ds(first, rows), place], texts[pl.ds(first, rows), :], TN, preferred_element_type=jnp.float32
         )
         if first:
-            image_part[lanes, :] += part
-        else:
-            image_part[lanes, :] = part
+            part = image_part[place, :] + part
+        image_part[place, :] = part
 
     def pack_text(row, rows):
         text_send[pl.ds(row - ROWS, rows), :] = packed(text_part[pl.ds(row, rows), :])
@@ -145,27 +147,49 @@
     forward_z(0, (0, 1))
     forward_y(1)
     y_last = (send(right, texts, HALF, texts, 960, HALF), send(left, texts, 0, texts, 1120, HALF))
-    forward_z(0, (2, 3))
     n_image.wait_recv()
-    coefficients(0, 0)
-    forward_z(1, (0,))
-    coefficients(1, 0)
-    forward_z(1, (1, 2))
-    for copy in y_far[0]:
-        copy.wait_recv()
-    forward_z(1, (3,))
-    for copy in y_far[1]:
-        copy.wait_recv()
-    coefficients(2, 0)
+    coefficients(0, 0, 640)
+    coefficients(1, 0, 640)
+    forward_z(0, (2,))
+    forward_z(1, (0, 1))
+    text_rows(1, 0)
+    text_rows(0, 0)
+    image_rows(0, 640, 0, 2 * ROWS)
+    forward_z(0, (3,))
+    forward_z(1, (2, 3))
+    coefficients(1, 640, 256)
+    coefficients(0, 640, 256)
+    for i in range(2):
+        for copy in y_far[i]:
+            copy.wait_recv()
+    coefficients(2, 0, 640)
+    coefficients(2, 640, 256)
     for copy in nz_image:
         copy.wait_recv()
 
-    coefficients(1, 1)
-    text_rows(1)
+    coefficients(1, 896, 384)
+    text_rows(1, 1)
     pack_text(320, ROWS)
-    near = [(send(left, text_send, 0, right_recv, 0, PIECE), send(right, text_send, 160, left_recv, 160, PIECE))]
-    coefficients(2, 1)
-    text_rows(2)
+    near = [
+        (
+            send(left, text_send, PIECE * i, right_recv, PIECE * i, PIECE),
+            send(right, text_send, HALF + PIECE * i, left_recv, HALF + PIECE * i, PIECE),
+        )
+        for i in range(2)
+    ]
+    coefficients(2, 896, 384)
+    coefficients(0, 896, 384)
+    image_rows(896, 384, 0, 3 * ROWS)
+    image_rows(640, 256, 0, 3 * ROWS)
+    for copy in y_last:
+        copy.wait_recv()
+    coefficients(3, 640, 640)
+    image_rows(896, 384, 3 * ROWS, ROWS)
+    image_send[pl.ds(640, ROWS), :] = packed(image_part[pl.ds(960, ROWS), :])
+    nz_part = [send(after, image_send, 640 + PIECE * i, zn_recv, PIECE * i, PIECE) for i in range(4)]
+    image_rows(640, 256, 3 * ROWS, ROWS)
+    text_rows(2, 0)
+    text_rows(2, 1)
     pack_text(640, ROWS)
     mid = []
     for i in range(2):
@@ -173,31 +197,19 @@
             send(left, text_send, 480 + PIECE * i, mid_recv, PIECE * i, PIECE),
             send(right, text_send, 320 + PIECE * i, mid_recv, HALF + PIECE * i, PIECE),
         ))
-    near.append((send(left, text_send, PIECE, right_recv, PIECE, PIECE), send(right, text_send, 240, left_recv, 240, PIECE)))
-    coefficients(0, 1)
-    image_rows(1, 0, 3 * ROWS)
-    for copy in y_last:
-        copy.wait_recv()
-    coefficients(3, 1)
-    image_rows(1, 3 * ROWS, ROWS)
-    image_send[pl.ds(640, ROWS), :] = packed(image_part[pl.ds(960, ROWS), :])
-    nz_part = [send(after, image_send, 640 + PIECE * i, zn_recv, PIECE * i, PIECE) for i in range(4)]
-    coefficients(3, 0)
-    image_rows(0, 0, BLOCK)
-    image_send[pl.ds(0, ROWS), :] = packed(image_part[pl.ds(320, ROWS), :])
-    n_part = send(after, image_send, 0, dn_recv, 0, ROWS)
-    text_rows(3)
-    text_rows(0)
-
-    z_part, last = [], []
-
-    def reduce_z(i):
-        nz_part[i].wait_recv()
-        rows = pl.ds(PIECE * i, PIECE)
-        image_send[pl.ds(320 + PIECE * i, PIECE), :] = packed(
-            image_part[pl.ds(640 + PIECE * i, PIECE), :] + unpacked(zn_recv[rows, :])
-        )
-        z_part.append(send(partner, image_send, 320 + PIECE * i, z_recv, PIECE * i, PIECE))
+    z_part = [send(partner, image_send, 320 + PIECE * i, z_recv, PIECE * i, PIECE, False) for i in range(4)]
+    last = []
+
+    def reduce_z(which, pieces):
+        @pl.when(core == which)
+        def _():
+            for i in pieces:
+                nz_part[i].wait_recv()
+                rows = pl.ds(PIECE * i, PIECE)
+                image_send[pl.ds(320 + PIECE * i, PIECE), :] = packed(
+                    image_part[pl.ds(640 + PIECE * i, PIECE), :] + unpacked(zn_recv[rows, :])
+                )
+                z_part[i].start()
 
     def reduce_y(i):
         pair = []
@@ -210,11 +222,18 @@
             pair.append(send(device, text_send, 640 + row, target, target_row + PIECE * i, PIECE))
         last.append(pair)
 
-    reduce_z(0)
-    reduce_z(1)
+    reduce_z(1, range(4))
+    coefficients(3, 0, 640)
+    image_rows(0, 640, 2 * ROWS, 2 * ROWS)
+    image_send[pl.ds(0, ROWS), :] = packed(image_part[pl.ds(320, ROWS), :])
+    n_part = send(after, image_send, 0, dn_recv, 0, ROWS)
+    reduce_z(0, (0,))
+    text_rows(3, 0)
+    text_rows(3, 1)
+    reduce_z(0, (1,))
+    text_rows(0, 1)
+    reduce_z(0, (2, 3))
     reduce_y(0)
-    reduce_z(2)
-    reduce_z(3)
     reduce_y(1)
 
     n_part.wait_recv()

time: 65.1 us -> 61.1 us (0.939)
  Pallas kernels: 60.8 us -> 56.8 us
    pallas_call x1, Pallas kernels: 60.8 us -> 56.8 us  [per_device(): pl.pallas_call(kernel, out_shape=(out, out), in_specs=[pl.BlockSpec(memor...]
where the time goes in v3:
time: 61.1 us; the launch traced here: 61 us
  Pallas kernels  56.8 us (93%)
  local copies, waits for them, and re-layouts  2.22 us (4%)
  between operations  1.93 us (3%)
    pallas_call x1, Pallas kernels, per_device(): pl.pallas_call(kernel, out_shape=(out, out), in_specs=[pl.BlockSpec(memor...  56.8 us
    unnamed x2, local copies, waits for them, and re-layouts  2.22 us

profile of v3, /device:TPU:0, one launch (start us, length us, event | category | flops | bytes accessed | tf_op | source)
XLA Modules:
  0.0 61.0 jit_solution(3779879089547714192)
XLA Ops:
  1.9 56.8 %shard_map.59 = (f32[320,1152]{1,0:T(8,128)S(1)}, f32[320,1152]{1,0:T(8,128)S(1)}) custom-call(f32[1]{0:T(128)} %bitcast.2.scale_ref, f32[1]{0:T(128)} %bitcast.3.bias_ref, f32[320,1152]{1,0:T(8,128)} %image_hbm.1, f32[320,1152]{1,0:T(8,128)} %text_hbm.1), custom_call_target="tpu_custom_call" | custom-call | flops 11324620800 | bytes 5898240 | tf_op jit(solution)/shard_map/pallas_call | solution.py:265
  58.8 1.1 %copy.8 = f32[320,1152]{1,0:T(8,128)} copy(f32[320,1152]{1,0:T(8,128)S(1)} %get-tuple-element.2) | data formatting | bytes 2949120
  59.9 1.1 %copy.9 = f32[320,1152]{1,0:T(8,128)} copy(f32[320,1152]{1,0:T(8,128)S(1)} %get-tuple-element.3) | data formatting | bytes 2949120

commit v4 on v3

--- a/solution.py
+++ b/solution.py
@@ -180,25 +180,15 @@
     coefficients(2, 896, 384)
     coefficients(0, 896, 384)
     image_rows(896, 384, 0, 3 * ROWS)
-    image_rows(640, 256, 0, 3 * ROWS)
     for copy in y_last:
         copy.wait_recv()
     coefficients(3, 640, 640)
     image_rows(896, 384, 3 * ROWS, ROWS)
     image_send[pl.ds(640, ROWS), :] = packed(image_part[pl.ds(960, ROWS), :])
     nz_part = [send(after, image_send, 640 + PIECE * i, zn_recv, PIECE * i, PIECE) for i in range(4)]
-    image_rows(640, 256, 3 * ROWS, ROWS)
+    image_rows(640, 256, 0, BLOCK)
     text_rows(2, 0)
-    text_rows(2, 1)
-    pack_text(640, ROWS)
-    mid = []
-    for i in range(2):
-        mid.append((
-            send(left, text_send, 480 + PIECE * i, mid_recv, PIECE * i, PIECE),
-            send(right, text_send, 320 + PIECE * i, mid_recv, HALF + PIECE * i, PIECE),
-        ))
     z_part = [send(partner, image_send, 320 + PIECE * i, z_recv, PIECE * i, PIECE, False) for i in range(4)]
-    last = []
 
     def reduce_z(which, pieces):
         @pl.when(core == which)
@@ -211,6 +201,17 @@
                 )
                 z_part[i].start()
 
+    reduce_z(1, range(4))
+    text_rows(2, 1)
+    pack_text(640, ROWS)
+    mid = []
+    for i in range(2):
+        mid.append((
+            send(left, text_send, 480 + PIECE * i, mid_recv, PIECE * i, PIECE),
+            send(right, text_send, 320 + PIECE * i, mid_recv, HALF + PIECE * i, PIECE),
+        ))
+    last = []
+
     def reduce_y(i):
         pair = []
         for k, device, target, target_row in ((0, left, right_recv, HALF), (1, right, left_recv, 0)):
@@ -222,7 +223,6 @@
             pair.append(send(device, text_send, 640 + row, target, target_row + PIECE * i, PIECE))
         last.append(pair)
 
-    reduce_z(1, range(4))
     coefficients(3, 0, 640)
     image_rows(0, 640, 2 * ROWS, 2 * ROWS)
     image_send[pl.ds(0, ROWS), :] = packed(image_part[pl.ds(320, ROWS), :])
@@ -257,12 +257,23 @@
         copy.wait_send()
 
 
+def finish(image_ref, text_ref, image_out, text_out, sem):
+    copies = [
+        pltpu.make_async_copy(source, target, sem.at[k])
+        for k, (source, target) in enumerate(((image_ref, image_out), (text_ref, text_out)))
+    ]
+    for copy in copies:
+        copy.start()
+    for copy in copies:
+        copy.wait()
+
+
 def per_device(image_embed, text_embed, logit_scale, logit_bias):
     half = lambda rows: pltpu.VMEM((rows, WIDTH), jnp.bfloat16)
     full = lambda rows: pltpu.VMEM((rows, WIDTH), jnp.float32)
     n_copies = 48
     out = pltpu.VMEM((ROWS, WIDTH), jnp.float32)
-    return pl.pallas_call(
+    sums = pl.pallas_call(
         kernel,
         out_shape=(out, out),
         in_specs=[pl.BlockSpec(memory_space=pltpu.SMEM)] * 2 + [pl.BlockSpec(memory_space=pltpu.HBM)] * 2,
@@ -281,6 +292,16 @@
             flops=6 * BLOCK * BLOCK * WIDTH, bytes_accessed=16 * ROWS * WIDTH, transcendentals=BLOCK * BLOCK
         ),
     )(logit_scale.reshape(1), logit_bias.reshape(1), image_embed, text_embed)
+    result = jax.ShapeDtypeStruct((ROWS, WIDTH), jnp.float32)
+    return pl.pallas_call(
+        finish,
+        out_shape=(result, result),
+        in_specs=[pl.BlockSpec(memory_space=pl.ANY)] * 2,
+        out_specs=(pl.BlockSpec(memory_space=pl.ANY),) * 2,
+        scratch_shapes=[pltpu.SemaphoreType.DMA((2,))],
+        compiler_params=pltpu.CompilerParams(vmem_limit_bytes=2**20),
+        cost_estimate=pl.CostEstimate(flops=0, bytes_accessed=16 * ROWS * WIDTH, transcendentals=0),
+    )(*sums)
 
 
 def solution(mesh):

time: 61.1 us -> 60.2 us (0.985)
  local copies, waits for them, and re-layouts: 2.22 us -> 0 us
  Pallas kernels: 56.8 us -> 58 us
    unnamed x2 -> x0, local copies, waits for them, and re-layouts: 2.22 us -> none
    pallas_call x0 -> x1, Pallas kernels: none -> 1.61 us  [per_device(): pl.pallas_call(finish, out_shape=(result, result), in_specs=[pl.BlockSpec...]
where the time goes in v4:
time: 60.2 us; the launch traced here: 60.1 us
  Pallas kernels  58 us (96%)
  between operations  2.09 us (3%)
    pallas_call x1, Pallas kernels, per_device(): pl.pallas_call(kernel, out_shape=(out, out), in_specs=[pl.BlockSpec(memor...  56.4 us
    pallas_call x1, Pallas kernels, per_device(): pl.pallas_call(finish, out_shape=(result, result), in_specs=[pl.BlockSpec...  1.61 us

profile of v4, /device:TPU:0, one launch (start us, length us, event | category | flops | bytes accessed | tf_op | source)
XLA Modules:
  0.0 60.1 jit_solution(15638870815978392274)
XLA Ops:
  1.9 56.4 %shard_map.59 = (f32[320,1152]{1,0:T(8,128)S(1)}, f32[320,1152]{1,0:T(8,128)S(1)}) custom-call(f32[1]{0:T(128)} %bitcast.2.scale_ref, f32[1]{0:T(128)} %bitcast.3.bias_ref, f32[320,1152]{1,0:T(8,128)} %image_hbm.1, f32[320,1152]{1,0:T(8,128)} %text_hbm.1), custom_call_target="tpu_custom_call" | custom-call | flops 11324620800 | bytes 5898240 | tf_op jit(solution)/shard_map/pallas_call | solution.py:276
  58.3 1.6 %shard_map.60 = (f32[320,1152]{1,0:T(8,128)}, f32[320,1152]{1,0:T(8,128)}) custom-call(f32[320,1152]{1,0:T(8,128)S(1)} %get-tuple-element.4.image_ref, f32[320,1152]{1,0:T(8,128)S(1)} %get-tuple-element.5.text_ref), custom_call_target="tpu_custom_call" | custom-call | bytes 5898240 | tf_op jit(solution)/shard_map/pallas_call | solution.py:296

commit v5 on v4

--- a/solution.py
+++ b/solution.py
@@ -164,6 +164,7 @@
             copy.wait_recv()
     coefficients(2, 0, 640)
     coefficients(2, 640, 256)
+    text_rows(2, 0)
     for copy in nz_image:
         copy.wait_recv()
 
@@ -187,7 +188,6 @@
     image_send[pl.ds(640, ROWS), :] = packed(image_part[pl.ds(960, ROWS), :])
     nz_part = [send(after, image_send, 640 + PIECE * i, zn_recv, PIECE * i, PIECE) for i in range(4)]
     image_rows(640, 256, 0, BLOCK)
-    text_rows(2, 0)
     z_part = [send(partner, image_send, 320 + PIECE * i, z_recv, PIECE * i, PIECE, False) for i in range(4)]
 
     def reduce_z(which, pieces):
@@ -234,25 +234,32 @@
     text_rows(0, 1)
     reduce_z(0, (2, 3))
     reduce_y(0)
-    reduce_y(1)
-
-    n_part.wait_recv()
-    image_out[...] = image_part[pl.ds(0, ROWS), :] + unpacked(dn_recv[...])
-    for i in range(2):
-        for j in (2 * i, 2 * i + 1):
-            z_part[j].wait_recv()
-        rows = pl.ds(HALF * i, HALF)
-        image_out[rows, :] += unpacked(z_recv[rows, :])
+    image_out[...] = image_part[pl.ds(0, ROWS), :]
     for pair in near:
         for copy in pair:
             copy.wait_recv()
     text_out[pl.ds(0, HALF), :] = text_part[pl.ds(0, HALF), :] + unpacked(right_recv[pl.ds(0, HALF), :])
     text_out[pl.ds(HALF, HALF), :] = text_part[pl.ds(HALF, HALF), :] + unpacked(left_recv[pl.ds(HALF, HALF), :])
-    for i in range(2):
+    reduce_y(1)
+
+    def add_image(i):
+        rows = pl.ds(HALF * i, HALF)
+        for j in (2 * i, 2 * i + 1):
+            z_part[j].wait_recv()
+        image_out[rows, :] += unpacked(z_recv[rows, :])
+
+    def add_text(i):
         for k, source, row in ((0, right_recv, HALF), (1, left_recv, 0)):
             last[i][k].wait_recv()
             rows = pl.ds(row + PIECE * i, PIECE)
             text_out[rows, :] += unpacked(source[rows, :])
+
+    add_image(0)
+    add_text(0)
+    n_part.wait_recv()
+    image_out[...] += unpacked(dn_recv[...])
+    add_image(1)
+    add_text(1)
     for copy in copies:
         copy.wait_send()
 

time: 60.2 us -> 59.8 us (level)
  no operation moved by 1% of the time
where the time goes in v5:
time: 59.8 us; the launch traced here: 59.6 us
  Pallas kernels  57.5 us (96%)
  between operations  2.09 us (3%)
    pallas_call x1, Pallas kernels, per_device(): pl.pallas_call(kernel, out_shape=(out, out), in_specs=[pl.BlockSpec(memor...  55.9 us
    pallas_call x1, Pallas kernels, per_device(): pl.pallas_call(finish, out_shape=(result, result), in_specs=[pl.BlockSpec...  1.61 us

profile of v5, /device:TPU:0, one launch (start us, length us, event | category | flops | bytes accessed | tf_op | source)
XLA Modules:
  0.0 59.6 jit_solution(3390942114174923073)
XLA Ops:
  1.9 55.9 %shard_map.59 = (f32[320,1152]{1,0:T(8,128)S(1)}, f32[320,1152]{1,0:T(8,128)S(1)}) custom-call(f32[1]{0:T(128)} %bitcast.2.scale_ref, f32[1]{0:T(128)} %bitcast.3.bias_ref, f32[320,1152]{1,0:T(8,128)} %image_hbm.1, f32[320,1152]{1,0:T(8,128)} %text_hbm.1), custom_call_target="tpu_custom_call" | custom-call | flops 11324620800 | bytes 5898240 | tf_op jit(solution)/shard_map/pallas_call | solution.py:283
  57.8 1.6 %shard_map.60 = (f32[320,1152]{1,0:T(8,128)}, f32[320,1152]{1,0:T(8,128)}) custom-call(f32[320,1152]{1,0:T(8,128)S(1)} %get-tuple-element.4.image_ref, f32[320,1152]{1,0:T(8,128)S(1)} %get-tuple-element.5.text_ref), custom_call_target="tpu_custom_call" | custom-call | bytes 5898240 | tf_op jit(solution)/shard_map/pallas_call | solution.py:303

commit v6 on v5

--- a/solution.py
+++ b/solution.py
@@ -142,8 +142,8 @@
         b = send(left, texts, 480 + PIECE * i, texts, 800 + PIECE * i, PIECE)
         y_far.append((a, b))
 
+    start_z(1)
     forward_y(0)
-    start_z(1)
     forward_z(0, (0, 1))
     forward_y(1)
     y_last = (send(right, texts, HALF, texts, 960, HALF), send(left, texts, 0, texts, 1120, HALF))

time: 59.8 us -> 59.8 us (level)
  no operation moved by 1% of the time
where the time goes in v6:
time: 59.8 us; the launch traced here: 59.6 us
  Pallas kernels  57.5 us (96%)
  between operations  2.09 us (3%)
    pallas_call x1, Pallas kernels, per_device(): pl.pallas_call(kernel, out_shape=(out, out), in_specs=[pl.BlockSpec(memor...  55.9 us
    pallas_call x1, Pallas kernels, per_device(): pl.pallas_call(finish, out_shape=(result, result), in_specs=[pl.BlockSpec...  1.61 us

profile of v6, /device:TPU:0, one launch (start us, length us, event | category | flops | bytes accessed | tf_op | source)
XLA Modules:
  0.0 59.6 jit_solution(16785352494557210995)
XLA Ops:
  1.9 55.9 %shard_map.59 = (f32[320,1152]{1,0:T(8,128)S(1)}, f32[320,1152]{1,0:T(8,128)S(1)}) custom-call(f32[1]{0:T(128)} %bitcast.2.scale_ref, f32[1]{0:T(128)} %bitcast.3.bias_ref, f32[320,1152]{1,0:T(8,128)} %image_hbm.1, f32[320,1152]{1,0:T(8,128)} %text_hbm.1), custom_call_target="tpu_custom_call" | custom-call | flops 11324620800 | bytes 5898240 | tf_op jit(solution)/shard_map/pallas_call | solution.py:283
  57.8 1.6 %shard_map.60 = (f32[320,1152]{1,0:T(8,128)}, f32[320,1152]{1,0:T(8,128)}) custom-call(f32[320,1152]{1,0:T(8,128)S(1)} %get-tuple-element.4.image_ref, f32[320,1152]{1,0:T(8,128)S(1)} %get-tuple-element.5.text_ref), custom_call_target="tpu_custom_call" | custom-call | bytes 5898240 | tf_op jit(solution)/shard_map/pallas_call | solution.py:303
